TPU v7x, 32 devices: a whole 2x2x4 slice. The times are simulated.
32 devices in a mesh: dp: 8 (over z, x), seq: 4 (over y, core).
Axes of the slice: x: 2, y: 2, z: 4, core: 2. Of those that a mesh axis runs over, the one named last changes fastest.
Arguments:
- hidden_in: bfloat16 [16384, 576], P(('dp', 'seq')), may hold values from -6 to 6
- span_order: int32 [128], P(('dp', 'seq')), may hold values from 0 to 3, as said below
- attention_norm_gain: bfloat16 [576], replicated, may hold values from 0.5 to 1.5
- query_weight: bfloat16 [331776], P(('dp', 'seq')), may hold values from -0.5 to 0.5
- key_weight: bfloat16 [110592], P(('dp', 'seq')), may hold values from -0.25 to 0.25
- value_weight: bfloat16 [110592], P(('dp', 'seq')), may hold values from -0.25 to 0.25
- output_weight: bfloat16 [331776], P(('dp', 'seq')), may hold values from -2 to 2
- feedforward_gain: bfloat16 [576], replicated, may hold values from 0.5 to 1.5
- gate_weight: bfloat16 [884736], P(('dp', 'seq')), may hold values from -0.25 to 0.25
- up_weight: bfloat16 [884736], P(('dp', 'seq')), may hold values from -0.25 to 0.25
- down_weight: bfloat16 [884736], P(('dp', 'seq')), may hold values from -0.15625 to 0.15625
- out_grad: bfloat16 [16384, 576], P(('dp', 'seq')), may hold values from -6 to 6
Outputs:
- hidden_out: bfloat16 [16384, 576], P(('dp', 'seq'))
- hidden_grad: bfloat16 [16384, 576], P(('dp', 'seq'))
- attn_gain_grad: float32 [576], replicated
- w_query_grad: float32 [331776], P(('dp', 'seq'))
- w_key_grad: float32 [110592], P(('dp', 'seq'))
- w_value_grad: float32 [110592], P(('dp', 'seq'))
- w_out_grad: float32 [331776], P(('dp', 'seq'))
- ffn_gain_grad: float32 [576], replicated
- w_gate_grad: float32 [884736], P(('dp', 'seq'))
- w_up_grad: float32 [884736], P(('dp', 'seq'))
- w_down_grad: float32 [884736], P(('dp', 'seq'))
Inputs may be any that keep to these rules, and one draw needn't show every extreme that they name: `span_order`: for each micro-batch and each group of 4 devices along seq that share a dp index, that micro-batch's entries on those devices are a permutation of 0 to 3.
All inputs are finite; a program needn't handle non-finite values.
Results may differ from a plain program's by a relative error of at most 0.015.
The roundings to bfloat16 on the way count: a program that leaves them out, or rounds other values in their place, can miss the bound.
Values may be sent and summed in bfloat16 or wider, within the bound.
No kernel may reach another device: no remote copies, remote signals or barrier semaphores. Data moves between devices by JAX's collectives and lax.ppermute only.
A program may use at most 128 MiB of HBM per device.

v0:
```python
import math

import jax
import jax.numpy as jnp
from jax import lax
from jax.sharding import PartitionSpec as P

MODEL_WIDTH = 576
QUERY_HEADS = 9
KEY_VALUE_HEADS = 3
HEAD_WIDTH = 64
HIDDEN_UNITS = 1536
SPAN = 128
MB = 4
SLOTS = 1


EPSILON = 1e-05


def angle_tables(positions, head_size):
    frequency = jnp.exp(
        jnp.arange(head_size // 2, dtype=jnp.float32) * (-2.0 * math.log(10000.0) / head_size)
    )
    angles = positions.astype(jnp.float32)[:, None] * frequency[None, :]
    angles = jnp.concatenate([angles, angles], axis=-1)[:, None, :]
    return (jnp.cos(angles), jnp.sin(angles))


def apply_rotation(value_rows, cosine_table, sine_values):
    half_size = value_rows.shape[-1] // 2
    turned = jnp.concatenate([-value_rows[..., half_size:], value_rows[..., :half_size]], axis=-1)
    return value_rows * cosine_table + turned * sine_values


def product(first_arg, second_arg):
    return jnp.dot(first_arg, second_arg, preferred_element_type=jnp.float32)


def inner_rows(first_arg, second_arg):
    return lax.dot_general(
        first_arg, second_arg, (((0,), (0,)), ((), ())), preferred_element_type=jnp.float32
    )


def inner_cols(first_arg, second_arg):
    return lax.dot_general(
        first_arg, second_arg, (((1,), (1,)), ((), ())), preferred_element_type=jnp.float32
    )


def shape_weights(flattened_rows):
    return (
        flattened_rows[0].reshape(MODEL_WIDTH, QUERY_HEADS * HEAD_WIDTH),
        flattened_rows[1].reshape(MODEL_WIDTH, KEY_VALUE_HEADS * HEAD_WIDTH),
        flattened_rows[2].reshape(MODEL_WIDTH, KEY_VALUE_HEADS * HEAD_WIDTH),
        flattened_rows[3].reshape(QUERY_HEADS * HEAD_WIDTH, MODEL_WIDTH),
        flattened_rows[4].reshape(MODEL_WIDTH, HIDDEN_UNITS),
        flattened_rows[5].reshape(MODEL_WIDTH, HIDDEN_UNITS),
        flattened_rows[6].reshape(HIDDEN_UNITS, MODEL_WIDTH),
    )


def block_scores(query_rows, key_block, query_place, key_place, factor):
    raw_scores = (
        jnp.einsum("qkgd,skd->kgqs", query_rows, key_block, preferred_element_type=jnp.float32)
        * factor
    )
    allowed = query_place[:, None] >= key_place[None, :]
    return jnp.where(allowed, raw_scores, -1e30)


def forward(layer_input, positions, span_ids, gain_pair, matrices):
    w_q, w_k, w_v, w_o, w_g, w_u, w_d = matrices
    count_of_rows = layer_input.shape[0]
    query_group_width = QUERY_HEADS // KEY_VALUE_HEADS
    factor = 1.0 / math.sqrt(HEAD_WIDTH)
    input_full = layer_input.astype(jnp.float32)
    scale_one = lax.rsqrt(jnp.mean(input_full * input_full, axis=-1, keepdims=True) + EPSILON)
    unit_one = input_full * scale_one
    normed = (unit_one * gain_pair[0]).astype(jnp.bfloat16)
    query_rows = product(normed, w_q)
    unrotated_keys = product(normed, w_k)
    value_rows = product(normed, w_v)
    cosine_table, sine_values = angle_tables(positions, HEAD_WIDTH)
    rotated_query = apply_rotation(
        query_rows.reshape(count_of_rows, QUERY_HEADS, HEAD_WIDTH), cosine_table, sine_values
    ).astype(jnp.bfloat16)
    rotated_query = rotated_query.reshape(
        count_of_rows, KEY_VALUE_HEADS, query_group_width, HEAD_WIDTH
    )
    rotated_key = apply_rotation(
        unrotated_keys.reshape(count_of_rows, KEY_VALUE_HEADS, HEAD_WIDTH),
        cosine_table,
        sine_values,
    ).astype(jnp.bfloat16)
    rotated_key = rotated_key.reshape(count_of_rows, KEY_VALUE_HEADS * HEAD_WIDTH)
    v_low = value_rows.astype(jnp.bfloat16)
    every_key, every_value, key_spans = (
        lax.all_gather(rotated_key, "seq", axis=0, tiled=True),
        lax.all_gather(v_low, "seq", axis=0, tiled=True),
        lax.all_gather(span_ids.astype(jnp.bfloat16), "seq", axis=0, tiled=True),
    )
    offsets = jnp.arange(SPAN, dtype=jnp.int32)
    key_places = (key_spans.astype(jnp.int32)[:, None] * SPAN + offsets[None, :]).reshape(-1)
    count_of_keys = every_key.shape[0]
    block_length = math.gcd(count_of_keys, 512)
    count_of_blocks = count_of_keys // block_length
    blocks_of_keys = every_key.reshape(count_of_blocks, block_length, KEY_VALUE_HEADS, HEAD_WIDTH)
    blocks_of_values = every_value.reshape(
        count_of_blocks, block_length, KEY_VALUE_HEADS, HEAD_WIDTH
    )
    place_blocks = key_places.reshape(count_of_blocks, block_length)

    def softmax_stats(carry, piece_set):
        highest, totals = carry
        key_block, key_place = piece_set
        scores = block_scores(rotated_query, key_block, positions, key_place, factor)
        new_high = jnp.maximum(highest, jnp.max(scores, axis=-1))
        totals = totals * jnp.exp(highest - new_high) + jnp.sum(
            jnp.exp(scores - new_high[..., None]), axis=-1
        )
        return ((new_high, totals), None)

    initial = (
        jnp.full((KEY_VALUE_HEADS, query_group_width, count_of_rows), -1e30, jnp.float32),
        jnp.zeros((KEY_VALUE_HEADS, query_group_width, count_of_rows), jnp.float32),
    )
    (highest, totals), _ = lax.scan(softmax_stats, initial, (blocks_of_keys, place_blocks))

    def mix_values(running, piece_set):
        key_block, value_block, key_place = piece_set
        scores = block_scores(rotated_query, key_block, positions, key_place, factor)
        layer_weights = (jnp.exp(scores - highest[..., None]) / totals[..., None]).astype(
            jnp.bfloat16
        )
        return (
            running
            + jnp.einsum(
                "kgqs,skd->qkgd", layer_weights, value_block, preferred_element_type=jnp.float32
            ),
            None,
        )

    attention_output, _ = lax.scan(
        mix_values,
        jnp.zeros((count_of_rows, KEY_VALUE_HEADS, query_group_width, HEAD_WIDTH), jnp.float32),
        (blocks_of_keys, blocks_of_values, place_blocks),
    )
    attention_output = attention_output.reshape(count_of_rows, QUERY_HEADS * HEAD_WIDTH)
    merged = attention_output.astype(jnp.bfloat16)
    middle = input_full + product(merged, w_o)
    scale_two = lax.rsqrt(jnp.mean(middle * middle, axis=-1, keepdims=True) + EPSILON)
    unit_two = middle * scale_two
    normed_two = (unit_two * gain_pair[1]).astype(jnp.bfloat16)
    gate_act = product(normed_two, w_g)
    upward = product(normed_two, w_u)
    hidden = (jax.nn.silu(gate_act) * upward).astype(jnp.bfloat16)
    result = (middle + product(hidden, w_d)).astype(jnp.bfloat16)
    stored = (
        scale_one,
        unit_one,
        normed,
        cosine_table,
        sine_values,
        rotated_query,
        blocks_of_keys,
        blocks_of_values,
        place_blocks,
        highest,
        totals,
        attention_output,
        merged,
        scale_two,
        unit_two,
        normed_two,
        gate_act,
        upward,
        hidden,
    )
    return (result, stored)


def backward(cotangent, positions, gain_pair, matrices, stored):
    w_q, w_k, w_v, w_o, w_g, w_u, w_d = matrices
    (
        scale_one,
        unit_one,
        normed,
        cosine_table,
        sine_values,
        rotated_query,
        blocks_of_keys,
        blocks_of_values,
        place_blocks,
        highest,
        totals,
        attention_output,
        merged,
        scale_two,
        unit_two,
        normed_two,
        gate_act,
        upward,
        hidden,
    ) = stored
    count_of_rows = cotangent.shape[0]
    query_group_width = QUERY_HEADS // KEY_VALUE_HEADS
    factor = 1.0 / math.sqrt(HEAD_WIDTH)
    grad_down = inner_rows(hidden, cotangent)
    back_hidden = inner_cols(cotangent, w_d)
    sigmoid_gate = jax.nn.sigmoid(gate_act)
    back_gate = (
        back_hidden * upward * sigmoid_gate * (1.0 + gate_act * (1.0 - sigmoid_gate))
    ).astype(jnp.bfloat16)
    back_up = (back_hidden * (gate_act * sigmoid_gate)).astype(jnp.bfloat16)
    grad_gate = inner_rows(normed_two, back_gate)
    grad_up = inner_rows(normed_two, back_up)
    back_norm_two = inner_cols(back_gate, w_g) + inner_cols(back_up, w_u)
    gain_two = jnp.sum(back_norm_two * unit_two, axis=0)
    back_unit = back_norm_two * gain_pair[1]
    back_middle = cotangent.astype(jnp.float32) + scale_two * (
        back_unit - unit_two * jnp.mean(back_unit * unit_two, axis=-1, keepdims=True)
    )
    middle_low = back_middle.astype(jnp.bfloat16)
    grad_out = inner_rows(merged, middle_low)
    attention_backward = inner_cols(middle_low, w_o).astype(jnp.bfloat16)
    head_gradient_rows = attention_backward.reshape(
        count_of_rows, KEY_VALUE_HEADS, query_group_width, HEAD_WIDTH
    )
    attention_head_rows = attention_output.reshape(
        count_of_rows, KEY_VALUE_HEADS, query_group_width, HEAD_WIDTH
    )
    correction = jnp.transpose(
        jnp.sum(head_gradient_rows.astype(jnp.float32) * attention_head_rows, axis=-1), (1, 2, 0)
    )

    def score_grads(running, piece_set):
        key_block, value_block, key_place = piece_set
        scores = block_scores(rotated_query, key_block, positions, key_place, factor)
        probs = jnp.exp(scores - highest[..., None]) / totals[..., None]
        back_probs = jnp.einsum(
            "qkgd,skd->kgqs", head_gradient_rows, value_block, preferred_element_type=jnp.float32
        )
        back_scores = (probs * (back_probs - correction[..., None])).astype(jnp.bfloat16)
        running = (
            running
            + jnp.einsum(
                "kgqs,skd->qkgd", back_scores, key_block, preferred_element_type=jnp.float32
            )
            * factor
        )
        key_grad = (
            jnp.einsum(
                "kgqs,qkgd->skd", back_scores, rotated_query, preferred_element_type=jnp.float32
            )
            * factor
        )
        value_grad = jnp.einsum(
            "kgqs,qkgd->skd",
            probs.astype(jnp.bfloat16),
            head_gradient_rows,
            preferred_element_type=jnp.float32,
        )
        return (running, (key_grad, value_grad))

    back_query, (gradient_of_keys, gradient_of_values) = lax.scan(
        score_grads,
        jnp.zeros((count_of_rows, KEY_VALUE_HEADS, query_group_width, HEAD_WIDTH), jnp.float32),
        (blocks_of_keys, blocks_of_values, place_blocks),
    )
    count_of_keys = gradient_of_keys.shape[0] * gradient_of_keys.shape[1]
    local_keys, value_own = (
        lax.psum_scatter(
            gradient_of_keys.reshape(count_of_keys, KEY_VALUE_HEADS * HEAD_WIDTH).astype(
                jnp.bfloat16
            ),
            "seq",
            scatter_dimension=0,
            tiled=True,
        ).astype(jnp.float32),
        lax.psum_scatter(
            gradient_of_values.reshape(count_of_keys, KEY_VALUE_HEADS * HEAD_WIDTH).astype(
                jnp.bfloat16
            ),
            "seq",
            scatter_dimension=0,
            tiled=True,
        ).astype(jnp.float32),
    )
    query_low = (
        apply_rotation(
            back_query.reshape(count_of_rows, QUERY_HEADS, HEAD_WIDTH), cosine_table, -sine_values
        )
        .astype(jnp.bfloat16)
        .reshape(count_of_rows, QUERY_HEADS * HEAD_WIDTH)
    )
    key_low = (
        apply_rotation(
            local_keys.reshape(count_of_rows, KEY_VALUE_HEADS, HEAD_WIDTH),
            cosine_table,
            -sine_values,
        )
        .astype(jnp.bfloat16)
        .reshape(count_of_rows, KEY_VALUE_HEADS * HEAD_WIDTH)
    )
    value_low = value_own.astype(jnp.bfloat16)
    grad_query = inner_rows(normed, query_low)
    grad_key = inner_rows(normed, key_low)
    grad_value = inner_rows(normed, value_low)
    back_norm_one = (
        inner_cols(query_low, w_q) + inner_cols(key_low, w_k) + inner_cols(value_low, w_v)
    )
    gain_one = jnp.sum(back_norm_one * unit_one, axis=0)
    back_unit_one = back_norm_one * gain_pair[0]
    input_back = back_middle + scale_one * (
        back_unit_one - unit_one * jnp.mean(back_unit_one * unit_one, axis=-1, keepdims=True)
    )
    weight_terms = (grad_query, grad_key, grad_value, grad_out, grad_gate, grad_up, grad_down)
    return (input_back.astype(jnp.bfloat16), weight_terms, (gain_one, gain_two))


def on_device(
    hidden_in,
    span_order,
    attention_norm_gain,
    query_weight,
    key_weight,
    value_weight,
    output_weight,
    feedforward_gain,
    gate_weight,
    up_weight,
    down_weight,
    out_grad,
):
    count_of_rows = SLOTS * SPAN
    gain_pair = (attention_norm_gain.astype(jnp.float32), feedforward_gain.astype(jnp.float32))
    offsets = jnp.arange(SPAN, dtype=jnp.int32)
    weight_totals = (
        jnp.zeros((MODEL_WIDTH, QUERY_HEADS * HEAD_WIDTH), jnp.float32),
        jnp.zeros((MODEL_WIDTH, KEY_VALUE_HEADS * HEAD_WIDTH), jnp.float32),
        jnp.zeros((MODEL_WIDTH, KEY_VALUE_HEADS * HEAD_WIDTH), jnp.float32),
        jnp.zeros((QUERY_HEADS * HEAD_WIDTH, MODEL_WIDTH), jnp.float32),
        jnp.zeros((MODEL_WIDTH, HIDDEN_UNITS), jnp.float32),
        jnp.zeros((MODEL_WIDTH, HIDDEN_UNITS), jnp.float32),
        jnp.zeros((HIDDEN_UNITS, MODEL_WIDTH), jnp.float32),
    )
    gain_totals = (jnp.zeros((MODEL_WIDTH,), jnp.float32), jnp.zeros((MODEL_WIDTH,), jnp.float32))
    outputs = []
    input_grads = []
    for micro_index in range(MB):
        layer_input = hidden_in[micro_index * count_of_rows : (micro_index + 1) * count_of_rows]
        cotangent = out_grad[micro_index * count_of_rows : (micro_index + 1) * count_of_rows]
        span_ids = span_order[micro_index * SLOTS : (micro_index + 1) * SLOTS]
        positions = (span_ids[:, None] * SPAN + offsets[None, :]).reshape(count_of_rows)
        forward_weights = shape_weights(
            (
                lax.all_gather(query_weight, ("dp", "seq"), axis=0, tiled=True),
                lax.all_gather(key_weight, ("dp", "seq"), axis=0, tiled=True),
                lax.all_gather(value_weight, ("dp", "seq"), axis=0, tiled=True),
                lax.all_gather(output_weight, ("dp", "seq"), axis=0, tiled=True),
                lax.all_gather(gate_weight, ("dp", "seq"), axis=0, tiled=True),
                lax.all_gather(up_weight, ("dp", "seq"), axis=0, tiled=True),
                lax.all_gather(down_weight, ("dp", "seq"), axis=0, tiled=True),
            )
        )
        result, stored = forward(layer_input, positions, span_ids, gain_pair, forward_weights)
        backward_weights = shape_weights(
            (
                lax.all_gather(query_weight, ("dp", "seq"), axis=0, tiled=True),
                lax.all_gather(key_weight, ("dp", "seq"), axis=0, tiled=True),
                lax.all_gather(value_weight, ("dp", "seq"), axis=0, tiled=True),
                lax.all_gather(output_weight, ("dp", "seq"), axis=0, tiled=True),
                lax.all_gather(gate_weight, ("dp", "seq"), axis=0, tiled=True),
                lax.all_gather(up_weight, ("dp", "seq"), axis=0, tiled=True),
                lax.all_gather(down_weight, ("dp", "seq"), axis=0, tiled=True),
            )
        )
        input_back, weight_terms, gain_terms = backward(
            cotangent, positions, gain_pair, backward_weights, stored
        )
        weight_totals = tuple(
            (running + term for running, term in zip(weight_totals, weight_terms))
        )
        gain_totals = tuple((running + term for running, term in zip(gain_totals, gain_terms)))
        outputs.append(result)
        input_grads.append(input_back)
    grad_query, grad_key, grad_value, grad_out, grad_gate, grad_up, grad_down = weight_totals
    owned = (
        lax.psum_scatter(grad_query.reshape(-1), ("dp", "seq"), scatter_dimension=0, tiled=True),
        lax.psum_scatter(grad_key.reshape(-1), ("dp", "seq"), scatter_dimension=0, tiled=True),
        lax.psum_scatter(grad_value.reshape(-1), ("dp", "seq"), scatter_dimension=0, tiled=True),
        lax.psum_scatter(grad_out.reshape(-1), ("dp", "seq"), scatter_dimension=0, tiled=True),
        lax.psum_scatter(grad_gate.reshape(-1), ("dp", "seq"), scatter_dimension=0, tiled=True),
        lax.psum_scatter(grad_up.reshape(-1), ("dp", "seq"), scatter_dimension=0, tiled=True),
        lax.psum_scatter(grad_down.reshape(-1), ("dp", "seq"), scatter_dimension=0, tiled=True),
    )
    gain_one, gain_two = lax.psum((gain_totals[0], gain_totals[1]), ("dp", "seq"))
    return (
        jnp.concatenate(outputs, axis=0),
        jnp.concatenate(input_grads, axis=0),
        gain_one,
        owned[0],
        owned[1],
        owned[2],
        owned[3],
        gain_two,
        owned[4],
        owned[5],
        owned[6],
    )


def solution(mesh):
    return jax.shard_map(
        on_device,
        mesh=mesh,
        in_specs=(
            P(("dp", "seq"), None),
            P(("dp", "seq")),
            P(),
            P(("dp", "seq")),
            P(("dp", "seq")),
            P(("dp", "seq")),
            P(("dp", "seq")),
            P(),
            P(("dp", "seq")),
            P(("dp", "seq")),
            P(("dp", "seq")),
            P(("dp", "seq"), None),
        ),
        out_specs=(
            P(("dp", "seq"), None),
            P(("dp", "seq"), None),
            P(),
            P(("dp", "seq")),
            P(("dp", "seq")),
            P(("dp", "seq")),
            P(("dp", "seq")),
            P(),
            P(("dp", "seq")),
            P(("dp", "seq")),
            P(("dp", "seq")),
        ),
        check_vma=False,
    )
```

profile of v0, /device:TPU:0, one launch (start us, length us, event | category | flops | bytes accessed | tf_op | source)
XLA Modules:
  0.0 813.8 jit_solution(287959642336638770)
XLA Ops:
  14.6 44.9 %all-gather = bf16[32,1,3456]{2,1,0:T(2,128)(2,1)S(1)} all-gather(bf16[1,1,3456]{2,1,0:T(2,128)(2,1)S(1)} %reshape.894), channel_id=1, replica_groups=mesh['dp'=8,'seq'=4] {'dp','seq'}, dimensions={0}, use_global_device_ids=true | all-gather | bytes 228096 | tf_op jit(solution)/shard_map/all_gather | solution.py:361
  62.9 38.0 %all-gather.1 = bf16[32,1,3456]{2,1,0:T(2,128)(2,1)S(1)} all-gather(bf16[1,1,3456]{2,1,0:T(2,128)(2,1)S(1)} %reshape.896), channel_id=1, replica_groups=mesh['dp'=8,'seq'=4] {'dp','seq'}, dimensions={0}, use_global_device_ids=true | all-gather | bytes 228096 | tf_op jit(solution)/shard_map/all_gather | solution.py:360
  106.6 43.0 %all-gather.2 = bf16[32,1,10368]{2,1,0:T(2,128)(2,1)S(1)} all-gather(bf16[1,1,10368]{2,1,0:T(2,128)(2,1)S(1)} %reshape.898), channel_id=1, replica_groups=mesh['dp'=8,'seq'=4] {'dp','seq'}, dimensions={0}, use_global_device_ids=true | all-gather | bytes 684288 | tf_op jit(solution)/shard_map/all_gather | solution.py:359
  149.7 4.8 reduce.2
  166.1 6.1 all_gather.54
  178.4 6.5 all-reduce.13
  187.0 5.8 all_gather.56
  196.2 41.9 %all-gather.3 = bf16[32,1,10368]{2,1,0:T(2,128)(2,1)S(1)} all-gather(bf16[1,1,10368]{2,1,0:T(2,128)(2,1)S(1)} %reshape.900), channel_id=1, replica_groups=mesh['dp'=8,'seq'=4] {'dp','seq'}, dimensions={0}, use_global_device_ids=true | all-gather | bytes 684288 | tf_op jit(solution)/shard_map/all_gather | solution.py:362
  238.1 4.8 reduce.3
  245.0 5.8 all_gather.51
  253.3 5.6 all_gather.53
  266.3 5.6 all_gather.48
  272.8 6.0 all_gather.50
  283.5 5.6 all_gather.39
  289.2 5.6 all_gather.42
  416.9 5.9 add_add_fusion.2
  450.9 6.6 add_add_fusion
  457.5 5.3 copy.80
  462.8 5.3 reshape.881
  476.9 13.2 %reduce-scatter.31.cloned.1.call-done = bf16[128,192]{1,0:T(8,128)(2,1)} async-done(((bf16[512,192]{1,0:T(8,128)(2,1)}), bf16[128,192]{1,0:T(8,128)(2,1)}) %reduce-scatter.31.cloned.1.call-update) | async-done | bytes 49168
  491.3 21.2 %reduce-scatter.35.cloned.1.call-done = bf16[128,192]{1,0:T(8,128)(2,1)} async-done(((bf16[512,192]{1,0:T(8,128)(2,1)}), bf16[128,192]{1,0:T(8,128)(2,1)}) %reduce-scatter.35.cloned.1.call-update) | async-done | bytes 49168
  513.6 21.5 %reduce-scatter.39.cloned.1.call-done = bf16[128,192]{1,0:T(8,128)(2,1)} async-done(((bf16[512,192]{1,0:T(8,128)(2,1)}), bf16[128,192]{1,0:T(8,128)(2,1)}) %reduce-scatter.39.cloned.1.call-update) | async-done | bytes 49168
  550.0 41.2 %all-reduce.11 = (f32[576]{0:T(1024)}, f32[576]{0:T(1024)}) all-reduce(f32[576]{0:T(1024)S(1)} %add_add_fusion.6, f32[576]{0:T(1024)S(1)} %add_add_fusion.5), channel_id=1, replica_groups=mesh['dp'=8,'seq'=4] {'dp','seq'}, use_global_device_ids=true, to_apply=%region_40.41 | all-reduce | flops 1152 | bytes 9216 | tf_op jit(solution)/shard_map/psum | solution.py:399
  593.5 202.8 %all-reduce.16.cloned.1.call-done = (f32[331776]{0:T(1024)}, f32[110592]{0:T(1024)}, f32[110592]{0:T(1024)}, f32[331776]{0:T(1024)}, f32[884736]{0:T(1024)}, /*index=5*/f32[884736]{0:T(1024)}, f32[884736]{0:T(1024)}) async-done(((f32[331776]{0:T(1024)}, f32[110592]{0:T(1024)}, f32[110592]{0:T(1024)}, f32[331776]{0:T(1024)}, f32[884736]{0:T(1024)}, /*index=5*/f32[884736]{0:T(1024)}, f32[884736]{0:T(1024)}), ...) | async-done | bytes 14155792
  (753 shorter events, 240.6 us)
Async XLA Ops:
  7.2 95.4 %copy-start.4 = (bf16[512,576]{0,1:T(8,128)(2,1)S(1)}, bf16[512,576]{0,1:T(8,128)(2,1)}, u32[]{:S(2)}) copy-start(bf16[512,576]{0,1:T(8,128)(2,1)} %param.12) | copy-start | bytes 1769476
  7.2 55.7 %copy-start.211 = (bf16[576]{0:T(1024)(128)(2,1)S(1)}, bf16[576]{0:T(1024)(128)(2,1)}, u32[]{:S(2)}) copy-start(bf16[576]{0:T(1024)(128)(2,1)} %param.14) | copy-start | bytes 3460
  7.2 55.7 %copy-start.197 = (bf16[3456]{0:T(1024)(128)(2,1)S(1)}, bf16[3456]{0:T(1024)(128)(2,1)}, u32[]{:S(2)}) copy-start(bf16[3456]{0:T(1024)(128)(2,1)} %param.16) | copy-start | bytes 20740
  7.2 293.6 %all-gather.8.cloned.1.call-start = ((), (), s32[]{:S(2)}) async-start(), calls=%async_computation.8 | async-start | bytes 1824768 | tf_op jit(solution)/shard_map/all_gather | solution.py:363
  7.9 296.5 %all-gather.10.cloned.1.call-start = ((), (), s32[]{:S(2)}) async-start(), calls=%async_computation.9 | async-start | bytes 1824768 | tf_op jit(solution)/shard_map/all_gather | solution.py:364
  8.7 303.1 %all-gather.12.cloned.1.call-start = ((), (), s32[]{:S(2)}) async-start(), calls=%async_computation.10 | async-start | bytes 1824768 | tf_op jit(solution)/shard_map/all_gather | solution.py:365
  9.4 458.9 %reduce-scatter.25.cloned.1.call-start = ((), (), s32[]{:S(2)}) async-start(), calls=%async_computation.11 | async-start | bytes 327680
  61.0 101.8 %copy-start.40 = (bf16[576,192]{1,0:T(8,128)(2,1)}, bf16[576,192]{1,0:T(8,128)(2,1)S(1)}, u32[]{:S(2)}) copy-start(bf16[576,192]{1,0:T(8,128)(2,1)S(1)} %reshape.844) | copy-start | bytes 663556
  62.9 43.7 %copy-start.182 = (bf16[10368]{0:T(1024)(128)(2,1)S(1)}, bf16[10368]{0:T(1024)(128)(2,1)}, u32[]{:S(2)}) copy-start(bf16[10368]{0:T(1024)(128)(2,1)} %param.15) | copy-start | bytes 62212
  62.9 94.0 %copy-start.188 = (f32[128]{0:T(128)}, f32[128]{0:T(128)S(1)}, u32[]{:S(2)}) copy-start(f32[128]{0:T(128)S(1)} %add_rsqrt_fusion.1) | copy-start | bytes 1540
  102.4 47.2 %copy-start.12 = (bf16[576,192]{1,0:T(8,128)(2,1)}, bf16[576,192]{1,0:T(8,128)(2,1)S(1)}, u32[]{:S(2)}) copy-start(bf16[576,192]{1,0:T(8,128)(2,1)S(1)} %reshape.845) | copy-start | bytes 663556
  102.6 57.5 %copy-start.155 = (bf16[192,576]{1,0:T(8,128)(2,1)}, bf16[192,576]{1,0:T(8,128)(2,1)S(1)}, u32[]{:S(2)}) copy-start(bf16[192,576]{1,0:T(8,128)(2,1)S(1)} %copy.60) | copy-start | bytes 663556
  104.6 52.7 %copy-start.192 = (f32[128]{0:T(128)}, f32[128]{0:T(128)S(1)}, u32[]{:S(2)}) copy-start(f32[128]{0:T(128)S(1)} %add_rsqrt_fusion.3) | copy-start | bytes 1540
  245.0 53.3 %copy-start = (bf16[576,576]{1,0:T(8,128)(2,1)}, bf16[576,576]{1,0:T(8,128)(2,1)S(1)}, u32[]{:S(2)}) copy-start(bf16[576,576]{1,0:T(8,128)(2,1)S(1)} %reshape.849) | copy-start | bytes 1990660
  355.3 114.1 %reduce-scatter.29.cloned.1.call-start = ((), (), s32[]{:S(2)}) async-start(), calls=%async_computation.13 | async-start | bytes 327680
  383.6 86.8 %reduce-scatter.33.cloned.1.call-start = ((), (), s32[]{:S(2)}) async-start(), calls=%async_computation.15 | async-start | bytes 327680
  391.3 80.1 %reduce-scatter.37.cloned.1.call-start = ((), (), s32[]{:S(2)}) async-start(), calls=%async_computation.17 | async-start | bytes 327680
  399.1 76.7 %reduce-scatter.27.cloned.1.call-start = ((), (), s32[]{:S(2)}) async-start(), calls=%async_computation.12 | async-start | bytes 327680
  405.1 85.1 %reduce-scatter.31.cloned.1.call-start = ((), (), s32[]{:S(2)}) async-start(), calls=%async_computation.14 | async-start | bytes 327680
  413.2 99.2 %reduce-scatter.35.cloned.1.call-start = ((), (), s32[]{:S(2)}) async-start(), calls=%async_computation.16 | async-start | bytes 327680
  450.8 84.3 %reduce-scatter.39.cloned.1.call-start = ((), (), s32[]{:S(2)}) async-start(), calls=%async_computation.18 | async-start | bytes 327680
  468.1 328.2 %all-reduce.16.cloned.1.call-start = ((), (), s32[]{:S(2)}) async-start(), calls=%async_computation.19 | async-start | bytes 28311552
  548.3 42.9 %copy-start.39 = (f32[128,576]{0,1:T(8,128)S(1)}, f32[128,576]{0,1:T(8,128)}, u32[]{:S(2)}) copy-start(f32[128,576]{0,1:T(8,128)} %copy-done.38) | copy-start | bytes 884740
  548.6 42.8 %copy-start.43 = (f32[128,576]{0,1:T(8,128)S(1)}, f32[128,576]{0,1:T(8,128)}, u32[]{:S(2)}) copy-start(f32[128,576]{0,1:T(8,128)} %copy-done.42) | copy-start | bytes 884740
  (211 other events, 932.3 us)
Sparse Core Ops, SparseCore 0:
  10.9 58.4 all-gather.7
  72.2 55.9 all-gather.9
  131.0 55.2 all-gather.11
  355.4 16.2 reduce-scatter.24
  383.7 16.1 reduce-scatter.28
  402.2 19.9 reduce-scatter.32
  424.9 20.0 reduce-scatter.36
  447.4 19.9 reduce-scatter.26
  470.0 20.0 reduce-scatter.30
  492.4 19.9 reduce-scatter.34
  515.1 20.0 reduce-scatter.38
  541.4 254.8 all-reduce.15
where the time goes:
time: 821 us; the launch traced here: 814 us
  blocking collectives  262 us (32%)
  waiting for transfers between devices  261 us (32%)
  matrix products  142 us (17%)
  local copies, waits for them, and re-layouts  88.3 us (11%)
  other arithmetic  40.1 us (5%)
  between operations  20.1 us (2%)
    unnamed x21, waiting for transfers between devices  261 us
    dot_general x28, matrix products, inner_rows(): lax.dot_general(first_arg, second_arg, (((0,), (0,)), ((), ())), preferre...  62.2 us
    all_gather x1, blocking collectives, on_device(): lax.all_gather(value_weight, ('dp', 'seq'), axis=0, tiled=True)  44.9 us
    unnamed x478, local copies, waits for them, and re-layouts  44.6 us
    all_gather x1, blocking collectives, on_device(): lax.all_gather(query_weight, ('dp', 'seq'), axis=0, tiled=True)  43 us
    all_gather x1, blocking collectives, on_device(): lax.all_gather(output_weight, ('dp', 'seq'), axis=0, tiled=True)  41.9 us
    psum x1, blocking collectives, on_device(): lax.psum((gain_totals[0], gain_totals[1]), ('dp', 'seq'))  41.2 us
    all_gather x1, blocking collectives, on_device(): lax.all_gather(key_weight, ('dp', 'seq'), axis=0, tiled=True)  38 us
  transfers between devices with their start and end apart: 12, of which 4 were waited for; matrix products, arithmetic and copies ran while one was open for 25% of the time, Pallas kernels for 0%

commit v1 on v0

--- a/solution.py
+++ b/solution.py
@@ -3,6 +3,8 @@
 import jax
 import jax.numpy as jnp
 from jax import lax
+from jax.experimental import pallas as pl
+from jax.experimental.pallas import tpu as pltpu
 from jax.sharding import PartitionSpec as P
 
 MODEL_WIDTH = 576
@@ -412,9 +414,654 @@
     )
 
 
+FACTOR = 1.0 / math.sqrt(HEAD_WIDTH)
+KV_WIDTH = KEY_VALUE_HEADS * HEAD_WIDTH
+Q_WIDTH = QUERY_HEADS * HEAD_WIDTH
+QK_WIDTH = Q_WIDTH + KV_WIDTH
+LANES = 128
+HALF_FFN = HIDDEN_UNITS // 2
+FFN_BLOCK = 256
+
+
+def vmem_params(megabytes=48):
+    return pltpu.CompilerParams(vmem_limit_bytes=megabytes * 1024 * 1024)
+
+
+def dot_nn(a, b):
+    return jnp.dot(a, b, preferred_element_type=jnp.float32)
+
+
+def dot_tn(a, b):
+    return lax.dot_general(a, b, (((0,), (0,)), ((), ())), preferred_element_type=jnp.float32)
+
+
+def dot_nt(a, b):
+    return lax.dot_general(a, b, (((1,), (1,)), ((), ())), preferred_element_type=jnp.float32)
+
+
+def low(v):
+    return v.astype(jnp.bfloat16)
+
+
+def place_back(v, place):
+    high = low(v)
+    rest = low(v - high.astype(jnp.float32))
+    return dot_nt(high, place) + dot_nt(rest, place)
+
+
+def half_turn(u, lane):
+    return jnp.where(
+        lane % HEAD_WIDTH < HEAD_WIDTH // 2,
+        pltpu.roll(u, LANES - HEAD_WIDTH // 2, 1),
+        pltpu.roll(u, HEAD_WIDTH // 2, 1),
+    )
+
+
+def padded_heads(blocks, head, lane):
+    here = blocks[head // 2]
+    moved = pltpu.roll(here, HEAD_WIDTH, 1)
+    low_half, high_half = (here, moved) if head % 2 == 0 else (moved, here)
+    zero = jnp.zeros_like(here)
+    return (
+        low(jnp.where(lane < HEAD_WIDTH, low_half, zero)),
+        low(jnp.where(lane >= HEAD_WIDTH, high_half, zero)),
+    )
+
+
+def attend_kernel(
+    spans, x0, x1, x2, x3, gain_one, gain_two, place, cosine, sine, wa, wa2, wb, wb2,
+    x_out, normed_out, qk_out, kpad_out, vpad_out, lse_out, attn_out, merged_out, middle_out, normed_two_out,
+    wqk, wov,
+):
+    rows = x_out.shape[0]
+    half = wa.shape[0]
+    for k, block in enumerate((x0, x1, x2, x3)):
+        x_out[pl.ds(pl.multiple_of(spans[k] * SPAN, SPAN), SPAN), :] = block[...]
+    wqk[:half] = wa[...]
+    wqk[half:] = wa2[...]
+    wov[:half] = wb[...]
+    wov[half:] = wb2[...]
+    x = x_out[...].astype(jnp.float32)
+    scale = lax.rsqrt(jnp.mean(x * x, axis=-1, keepdims=True) + EPSILON)
+    normed = low(x * scale * gain_one[...])
+    normed_out[...] = low(dot_nn(normed, place[...]))
+    lane = lax.broadcasted_iota(jnp.int32, (rows, LANES), 1)
+    cos, sin = cosine[...], sine[...]
+    k_blocks = []
+    for b in range(QK_WIDTH // LANES):
+        u = dot_nn(normed_out[...], wqk[:, b * LANES : (b + 1) * LANES])
+        turned = u * cos + half_turn(u, lane) * sin
+        turned = low(turned).astype(jnp.float32)
+        if (b + 1) * LANES > Q_WIDTH:
+            k_blocks.append(turned)
+        if (b + 1) * LANES <= Q_WIDTH:
+            turned = turned * FACTOR
+        elif b * LANES < Q_WIDTH:
+            turned = jnp.where(lane < Q_WIDTH - b * LANES, turned * FACTOR, turned)
+        qk_out[:, b * LANES : (b + 1) * LANES] = low(turned)
+    first_group = QUERY_HEADS - 2 * (Q_WIDTH // LANES)
+    for j in range(KEY_VALUE_HEADS):
+        lo, hi = padded_heads(k_blocks, j + first_group, lane)
+        kpad_out[2 * j] = lo
+        kpad_out[2 * j + 1] = hi
+    v = dot_nn(normed_out[...], wov[:, MODEL_WIDTH:])
+    v = low(v).astype(jnp.float32)
+    v = jnp.concatenate([v, jnp.zeros((rows, HEAD_WIDTH), jnp.float32)], axis=1)
+    v_blocks = [v[:, :LANES], v[:, LANES:]]
+    for j in range(KEY_VALUE_HEADS):
+        lo, hi = padded_heads(v_blocks, j, lane)
+        vpad_out[2 * j] = lo
+        vpad_out[2 * j + 1] = hi
+    lane_q = lax.broadcasted_iota(jnp.int32, (SPAN, LANES), 1)
+    diagonal = lax.broadcasted_iota(jnp.int32, (SPAN, SPAN), 0) >= lax.broadcasted_iota(
+        jnp.int32, (SPAN, SPAN), 1
+    )
+    groups = QUERY_HEADS // KEY_VALUE_HEADS
+    for i in range(rows // SPAN):
+        here = slice(i * SPAN, (i + 1) * SPAN)
+        lse = jnp.zeros((SPAN, LANES), jnp.float32)
+        for b in range((QUERY_HEADS + 1) // 2):
+            mixed = None
+            for h in range(2 * b, min(2 * b + 2, QUERY_HEADS)):
+                slot = 2 * (h // groups) + h % 2
+                q = qk_out[here, b * LANES : (b + 1) * LANES]
+                s = dot_nt(q, kpad_out[slot, : (i + 1) * SPAN, :])
+                s_last = jnp.where(diagonal, s[:, i * SPAN :], -1e30)
+                s = s_last if i == 0 else jnp.concatenate([s[:, : i * SPAN], s_last], axis=1)
+                top = jnp.max(s, axis=-1, keepdims=True)
+                p = jnp.exp(s - top)
+                total = jnp.sum(p, axis=-1, keepdims=True)
+                p = low(p * (1.0 / total))
+                lse = jnp.where(lane_q == h, top + jnp.log(total), lse)
+                part = dot_nn(p, vpad_out[slot, : (i + 1) * SPAN, :])
+                mixed = part if mixed is None else mixed + part
+            attn_out[here, b * LANES : (b + 1) * LANES] = mixed
+        lse_out[here, :] = lse
+    merged_out[...] = low(dot_nn(low(attn_out[:, :Q_WIDTH]), place[...]))
+    middle = x_out[...].astype(jnp.float32) + dot_nn(merged_out[...], wov[:, :MODEL_WIDTH])
+    middle_out[...] = middle
+    scale_two = lax.rsqrt(jnp.mean(middle * middle, axis=-1, keepdims=True) + EPSILON)
+    normed_two_out[...] = low(dot_nn(low(middle * scale_two * gain_two[...]), place[...]))
+
+
+def place_down_kernel(me, own, other, out, sems, *, order):
+    count = len(order)
+    rows = out.shape[0] // count
+    copies = []
+    for slot, relative in enumerate(order):
+        source = own if slot < count // 2 else other
+        at = slot % (count // 2)
+        target = pl.multiple_of((me[0] ^ relative) * rows, rows)
+        copies.append(
+            pltpu.make_async_copy(
+                source.at[pl.ds(at * rows, rows), :], out.at[pl.ds(target, rows), :], sems.at[slot]
+            )
+        )
+    for copy in copies:
+        copy.start()
+    for copy in copies:
+        copy.wait()
+
+
+def ffn_block(n2, og, wg, wu, wd, at, result, back_norm, dg_out, du_out, dd_out):
+    columns = pl.ds(pl.multiple_of(at * FFN_BLOCK, FFN_BLOCK), FFN_BLOCK)
+    half = dg_out[0].shape[0]
+    w_gate, w_up, w_down = wg[:, columns], wu[:, columns], wd[columns, :]
+    gate = dot_nn(n2, w_gate)
+    up = dot_nn(n2, w_up)
+    back_hidden = dot_nt(og, w_down)
+    sigmoid = jax.nn.sigmoid(gate)
+    silu = gate * sigmoid
+    hidden = low(silu * up)
+    back_gate = low(back_hidden * up * sigmoid * (1.0 + gate * (1.0 - sigmoid)))
+    back_up = low(back_hidden * silu)
+    dd_out[columns, :] = low(dot_tn(hidden, og))
+    dg = low(dot_tn(n2, back_gate))
+    du = low(dot_tn(n2, back_up))
+    dg_out[0][:, columns] = dg[:half]
+    dg_out[1][:, columns] = dg[half:]
+    du_out[0][:, columns] = du[:half]
+    du_out[1][:, columns] = du[half:]
+    result[...] += dot_nn(hidden, w_down)
+    back_norm[...] += dot_nt(back_gate, w_gate) + dot_nt(back_up, w_up)
+
+
+def ffn_first_kernel(
+    spans, o0, o1, o2, o3, n2, wg1, wg2, wu1, wu2, wd,
+    og_out, result_out, back_out, dg1, dg2, du1, du2, dd,
+    wg, wu,
+):
+    half = wg1.shape[0]
+    for k, block in enumerate((o0, o1, o2, o3)):
+        og_out[pl.ds(pl.multiple_of(spans[k] * SPAN, SPAN), SPAN), :] = block[...]
+    wg[:half] = wg1[...]
+    wg[half:] = wg2[...]
+    wu[:half] = wu1[...]
+    wu[half:] = wu2[...]
+    result_out[...] = jnp.zeros_like(result_out)
+    back_out[...] = jnp.zeros_like(back_out)
+
+    @pl.loop(0, HALF_FFN // FFN_BLOCK)
+    def _(at):
+        ffn_block(
+            n2[...], og_out[...], wg, wu, wd, at, result_out, back_out, (dg1, dg2), (du1, du2), dd
+        )
+
+
+def ffn_second_kernel(
+    me, spans, og, n2, wg1, wg2, wu1, wu2, wd, result_in, back_in, dd_in, middle, gain_two, place,
+    r0, r1, r2, r3, back_middle_out, gain_out, dg1, dg2, du1, du2, dd1, dd2,
+    wg, wu, dd, result, back, *, order,
+):
+    half = wg1.shape[0]
+    wg[:half] = wg1[...]
+    wg[half:] = wg2[...]
+    wu[:half] = wu1[...]
+    wu[half:] = wu2[...]
+    result[...] = result_in[...] + middle[...]
+    back[...] = back_in[...]
+
+    @pl.loop(0, HALF_FFN // FFN_BLOCK)
+    def _(at):
+        ffn_block(n2[...], og[...], wg, wu, wd, at, result, back, (dg1, dg2), (du1, du2), dd)
+
+    count = len(order)
+    rows = (dd_in.shape[0] + dd.shape[0]) // count
+    for slot, relative in enumerate(order):
+        owner = me[0] ^ relative
+        target = dd1 if slot < count // 2 else dd2
+        at = (slot % (count // 2)) * rows
+        first = owner < count // 2
+
+        @pl.when(first)
+        def _():
+            target[at : at + rows, :] = dd_in[pl.ds(pl.multiple_of(owner * rows, 16), rows), :]
+
+        @pl.when(jnp.logical_not(first))
+        def _():
+            target[at : at + rows, :] = dd[
+                pl.ds(pl.multiple_of((owner - count // 2) * rows, 16), rows), :
+            ]
+
+    for k, block in enumerate((r0, r1, r2, r3)):
+        block[...] = low(result[pl.ds(pl.multiple_of(spans[k] * SPAN, SPAN), SPAN), :])
+    mid = middle[...]
+    scale = lax.rsqrt(jnp.mean(mid * mid, axis=-1, keepdims=True) + EPSILON)
+    unit = mid * scale
+    back_norm = place_back(back[...], place[...])
+    gain_out[...] = jnp.sum(back_norm * unit, axis=0, keepdims=True)
+    back_unit = back_norm * gain_two[...]
+    back_middle_out[...] = og[...].astype(jnp.float32) + scale * (
+        back_unit - unit * jnp.mean(back_unit * unit, axis=-1, keepdims=True)
+    )
+
+
+def attend_back_kernel(
+    spans, x, normed, qk, kpad, vpad, lse, attn, merged, back_middle, gain_one, place, cosine, sine,
+    wa, wa2, wb, wb2,
+    g0, g1, g2, g3, gain_out, da1, da2, db1, db2,
+    wqk, wov, ab, dqk, dv, grad,
+):
+    rows = x.shape[0]
+    half = wa.shape[0]
+    wqk[:half] = wa[...]
+    wqk[half:] = wa2[...]
+    wov[:half] = wb[...]
+    wov[half:] = wb2[...]
+    middle_low = low(back_middle[...])
+    d_out = low(dot_tn(merged[...], middle_low))
+    db1[:, :MODEL_WIDTH] = d_out[:half]
+    db2[:, :MODEL_WIDTH] = d_out[half:]
+    ab_chunks = low(dot_nt(middle_low, wov[:, :MODEL_WIDTH]))
+    ab[:, :Q_WIDTH] = low(dot_nt(ab_chunks, place[...]))
+    ab[:, Q_WIDTH:] = jnp.zeros((rows, ab.shape[1] - Q_WIDTH), jnp.bfloat16)
+    terms = ab[...].astype(jnp.float32) * attn[...]
+    mask = low(
+        (
+            lax.broadcasted_iota(jnp.int32, (16, terms.shape[1]), 1) // HEAD_WIDTH
+            == lax.broadcasted_iota(jnp.int32, (16, terms.shape[1]), 0)
+        ).astype(jnp.float32)
+    )
+    high = low(terms)
+    correction = dot_nt(mask, high) + dot_nt(mask, low(terms - high.astype(jnp.float32)))
+    lse_rows = jnp.transpose(lse[...])
+    groups = QUERY_HEADS // KEY_VALUE_HEADS
+    diagonal = lax.broadcasted_iota(jnp.int32, (SPAN, SPAN), 1) >= lax.broadcasted_iota(
+        jnp.int32, (SPAN, SPAN), 0
+    )
+    lane = lax.broadcasted_iota(jnp.int32, (SPAN, LANES), 1)
+    for i in range(rows // SPAN):
+        keys = slice(i * SPAN, (i + 1) * SPAN)
+        first = i * SPAN
+        dk_sums = [None] * (2 * KEY_VALUE_HEADS)
+        dv_sums = [None] * (2 * KEY_VALUE_HEADS)
+        for b in range((QUERY_HEADS + 1) // 2):
+            columns = slice(b * LANES, (b + 1) * LANES)
+            q = qk[first:, columns]
+            a = ab[first:, columns]
+            dq = None
+            for h in range(2 * b, min(2 * b + 2, QUERY_HEADS)):
+                slot = 2 * (h // groups) + h % 2
+                s = dot_nt(kpad[slot, keys, :], q)
+                s = s - lse_rows[h : h + 1, first:]
+                s_first = jnp.where(diagonal, s[:, :SPAN], -1e30)
+                s = (
+                    s_first
+                    if first + SPAN == rows
+                    else jnp.concatenate([s_first, s[:, SPAN:]], axis=1)
+                )
+                p = jnp.exp(s)
+                dp = dot_nt(vpad[slot, keys, :], a)
+                ds = low(p * (dp - correction[h : h + 1, first:]))
+                dk = dot_nn(ds, q)
+                dvh = dot_nn(low(p), a)
+                dk_sums[slot] = dk if dk_sums[slot] is None else dk_sums[slot] + dk
+                dv_sums[slot] = dvh if dv_sums[slot] is None else dv_sums[slot] + dvh
+                part = dot_tn(ds, kpad[slot, keys, :])
+                dq = part if dq is None else dq + part
+            if i == 0:
+                dqk[first:, columns] = dq
+            else:
+                dqk[first:, columns] += dq
+
+        def both(sums, j):
+            even, odd = sums[2 * j], sums[2 * j + 1]
+            return even + pltpu.roll(odd, HEAD_WIDTH, 1)
+
+        dk_heads = [both(dk_sums, j) for j in range(KEY_VALUE_HEADS)]
+        dv_heads = [both(dv_sums, j) for j in range(KEY_VALUE_HEADS)]
+        key_scale = 1.0 / FACTOR
+        q_tail = dqk[keys, 4 * LANES : 5 * LANES]
+        dqk[keys, 4 * LANES : 5 * LANES] = jnp.where(
+            lane < HEAD_WIDTH, q_tail, pltpu.roll(dk_heads[0], HEAD_WIDTH, 1) * key_scale
+        )
+        dqk[keys, 5 * LANES :] = (
+            jnp.where(lane < HEAD_WIDTH, dk_heads[1], pltpu.roll(dk_heads[2], HEAD_WIDTH, 1))
+            * key_scale
+        )
+        dv[keys, :LANES] = low(
+            jnp.where(lane < HEAD_WIDTH, dv_heads[0], pltpu.roll(dv_heads[1], HEAD_WIDTH, 1))
+        )
+        dv[keys, LANES:] = low(dv_heads[2])
+    lane_all = lax.broadcasted_iota(jnp.int32, (rows, LANES), 1)
+    cos, sin = cosine[...], sine[...]
+    for b in range(QK_WIDTH // LANES):
+        u = dqk[:, b * LANES : (b + 1) * LANES] * FACTOR
+        grad[:, b * LANES : (b + 1) * LANES] = low(u * cos - half_turn(u, lane_all) * sin)
+    d_qk = low(dot_tn(normed[...], grad[...]))
+    da1[...] = d_qk[:half]
+    da2[...] = d_qk[half:]
+    dv_low = dv[:, :KV_WIDTH]
+    d_v = low(dot_tn(normed[...], dv_low))
+    db1[:, MODEL_WIDTH:] = d_v[:half]
+    db2[:, MODEL_WIDTH:] = d_v[half:]
+    back_chunks = dot_nt(grad[...], wqk[...]) + dot_nt(dv_low, wov[:, MODEL_WIDTH:])
+    back_norm = place_back(back_chunks, place[...])
+    xf = x[...].astype(jnp.float32)
+    scale = lax.rsqrt(jnp.mean(xf * xf, axis=-1, keepdims=True) + EPSILON)
+    unit = xf * scale
+    gain_out[...] = jnp.sum(back_norm * unit, axis=0, keepdims=True)
+    back_unit = back_norm * gain_one[...]
+    dqk[:, :MODEL_WIDTH] = back_middle[...] + scale * (
+        back_unit - unit * jnp.mean(back_unit * unit, axis=-1, keepdims=True)
+    )
+    for k, block in enumerate((g0, g1, g2, g3)):
+        block[...] = low(
+            dqk[pl.ds(pl.multiple_of(spans[k] * SPAN, SPAN), SPAN), :MODEL_WIDTH]
+        )
+
+
+VMEM_SPEC = pl.BlockSpec(memory_space=pltpu.VMEM)
+SMEM_SPEC = pl.BlockSpec(memory_space=pltpu.SMEM)
+ANY_SPEC = pl.BlockSpec(memory_space=pl.ANY)
+
+
+def shaped(rows, columns, kind):
+    return jax.ShapeDtypeStruct((rows, columns), kind)
+
+
+def call(body, outs, args, scalars, scratch, flops, megabytes=48):
+    return pl.pallas_call(
+        body,
+        out_shape=outs,
+        in_specs=[SMEM_SPEC] * scalars + [VMEM_SPEC] * (len(args) - scalars),
+        out_specs=[VMEM_SPEC] * len(outs),
+        scratch_shapes=scratch,
+        compiler_params=vmem_params(megabytes),
+        cost_estimate=pl.CostEstimate(
+            flops=int(flops), bytes_accessed=8_000_000, transcendentals=0
+        ),
+    )(*args)
+
+
+def whole_sequence_plan(mesh):
+    axes = ("dp", "seq")
+    n_dp, n_seq = mesh.shape["dp"], mesh.shape["seq"]
+    count = n_dp * n_seq
+    bits = count.bit_length() - 1
+    seq_bits = n_seq.bit_length() - 1
+    core, y_bit = 0, 1
+    x_bit = seq_bits
+    z_bits = tuple(range(seq_bits + 1, bits))[::-1]
+    order_bits = z_bits + (x_bit, y_bit, core)
+
+    def swap(v, bit):
+        return lax.ppermute(v, axes, [(d, d ^ (1 << bit)) for d in range(count)])
+
+    def relative(slot):
+        return sum(1 << bit for at, bit in enumerate(order_bits) if slot >> at & 1)
+
+    order = tuple(relative(slot) for slot in range(count))
+
+    def gather_z(v):
+        for bit in z_bits:
+            v = jnp.concatenate([v, swap(v, bit)], axis=0)
+        return v
+
+    def gather_xy(v, x_first):
+        if x_first:
+            v = jnp.concatenate([v, swap(v, x_bit)], axis=0)
+            v = jnp.concatenate([v, swap(v, y_bit)], axis=0)
+        else:
+            size = v.shape[0]
+            v = jnp.concatenate([v, swap(v, y_bit)], axis=0)
+            w = swap(v, x_bit)
+            v = jnp.concatenate([v[:size], w[:size], v[size:], w[size:]], axis=0)
+        return v, swap(v, core)
+
+    def gather_group(v):
+        v = gather_z(v)
+        half = v.shape[1] // 2
+        return gather_xy(v[:, :half], True) + gather_xy(v[:, half:], False)
+
+    def scatter_xy(keep, send, x_first):
+        total = keep.astype(jnp.float32) + swap(send, core).astype(jnp.float32)
+        size = total.shape[0] // 4
+        if x_first:
+            mine = jnp.concatenate([total[:size], total[2 * size : 3 * size]], axis=0)
+            theirs = jnp.concatenate([total[size : 2 * size], total[3 * size :]], axis=0)
+            total = mine + swap(low(theirs), x_bit).astype(jnp.float32)
+            return total[:size] + swap(low(total[size:]), y_bit).astype(jnp.float32)
+        total = total[: 2 * size] + swap(low(total[2 * size :]), y_bit).astype(jnp.float32)
+        return total[:size] + swap(low(total[size:]), x_bit).astype(jnp.float32)
+
+    def scatter_z(total):
+        for bit in z_bits[::-1]:
+            size = total.shape[0] // 2
+            total = total[:size] + swap(low(total[size:]), bit).astype(jnp.float32)
+        return total
+
+    def scatter_group(a, b):
+        total = jnp.concatenate([scatter_xy(*a, False), scatter_xy(*b, True)], axis=1)
+        return scatter_z(total)
+
+    def on_sequence_device(
+        hidden_in, span_order, attention_norm_gain, query_weight, key_weight, value_weight,
+        output_weight, feedforward_gain, gate_weight, up_weight, down_weight, out_grad,
+    ):
+        seq = lax.axis_index("seq")
+        me = lax.axis_index("dp") * n_seq + seq
+        rows = hidden_in.shape[0]
+        model_rows = MODEL_WIDTH // count
+        hidden_rows = HIDDEN_UNITS // count
+        gain_one = attention_norm_gain.astype(jnp.float32).reshape(1, MODEL_WIDTH)
+        gain_two = feedforward_gain.astype(jnp.float32).reshape(1, MODEL_WIDTH)
+
+        def to_sequence(blocks, size):
+            parts = [lax.dynamic_slice_in_dim(blocks, seq * size, size)]
+            for k in range(1, n_seq):
+                part = lax.dynamic_slice_in_dim(blocks, (seq ^ k) * size, size)
+                parts.append(
+                    lax.ppermute(part, "seq", [(d, d ^ k) for d in range(n_seq)])
+                )
+            return parts
+
+        def from_sequence(parts):
+            size = parts[0].shape[0]
+            out = jnp.zeros((size * n_seq,) + parts[0].shape[1:], parts[0].dtype)
+            for k, part in enumerate(parts):
+                if k:
+                    part = lax.ppermute(part, "seq", [(d, d ^ k) for d in range(n_seq)])
+                out = lax.dynamic_update_slice_in_dim(out, part, (seq ^ k) * size, 0)
+            return out
+
+        x_parts = to_sequence(hidden_in, SPAN)
+        spans = jnp.concatenate(to_sequence(span_order, 1))
+        def rows_of(w, columns):
+            return w.reshape(model_rows, columns)
+        first = jnp.concatenate(
+            [
+                rows_of(query_weight, Q_WIDTH),
+                rows_of(key_weight, KV_WIDTH),
+                rows_of(output_weight, MODEL_WIDTH),
+                rows_of(value_weight, KV_WIDTH),
+            ],
+            axis=1,
+        )
+        gate = rows_of(gate_weight, HIDDEN_UNITS)
+        up = rows_of(up_weight, HIDDEN_UNITS)
+        wa, wa2, wb, wb2 = gather_group(first)
+        down = gather_z(down_weight.reshape(hidden_rows, MODEL_WIDTH))
+        down, down2 = gather_xy(down, True)
+        ffn_weights = [
+            gather_group(
+                jnp.concatenate(
+                    [
+                        gate[:, c * HALF_FFN : (c + 1) * HALF_FFN],
+                        up[:, c * HALF_FFN : (c + 1) * HALF_FFN],
+                    ],
+                    axis=1,
+                )
+            )
+            for c in range(2)
+        ]
+        o_parts = to_sequence(out_grad, SPAN)
+
+        slots = jnp.asarray(order, jnp.int32)
+        natural = (
+            ((slots ^ me) * model_rows)[:, None] + jnp.arange(model_rows, dtype=jnp.int32)[None, :]
+        ).reshape(-1)
+        place = (jnp.arange(MODEL_WIDTH, dtype=jnp.int32)[:, None] == natural[None, :]).astype(
+            jnp.bfloat16
+        )
+        cosine, sine = angle_tables(jnp.arange(rows, dtype=jnp.int32), HEAD_WIDTH)
+        sign = jnp.where(jnp.arange(HEAD_WIDTH) < HEAD_WIDTH // 2, -1.0, 1.0)
+        cosine = jnp.tile(cosine[:, 0, :], (1, 2))
+        sine = jnp.tile(sine[:, 0, :] * sign, (1, 2))
+
+        bf, f4 = jnp.bfloat16, jnp.float32
+        half = MODEL_WIDTH // 2
+        me_scalar = me.reshape(1).astype(jnp.int32)
+        x, normed, qk, kpad, vpad, lse, attn, merged, middle, normed_two = call(
+            attend_kernel,
+            [
+                shaped(rows, MODEL_WIDTH, bf),
+                shaped(rows, MODEL_WIDTH, bf),
+                shaped(rows, QK_WIDTH, bf),
+                jax.ShapeDtypeStruct((2 * KEY_VALUE_HEADS, rows, LANES), bf),
+                jax.ShapeDtypeStruct((2 * KEY_VALUE_HEADS, rows, LANES), bf),
+                shaped(rows, LANES, f4),
+                shaped(rows, 5 * LANES, f4),
+                shaped(rows, Q_WIDTH, bf),
+                shaped(rows, MODEL_WIDTH, f4),
+                shaped(rows, MODEL_WIDTH, bf),
+            ],
+            [spans, *x_parts, gain_one, gain_two, place, cosine, sine, wa, wa2, wb, wb2],
+            1,
+            [pltpu.VMEM((MODEL_WIDTH, QK_WIDTH), bf), pltpu.VMEM((MODEL_WIDTH, QK_WIDTH), bf)],
+            4e9,
+        )
+        w_down = pl.pallas_call(
+            lambda *refs: place_down_kernel(*refs, order=order),
+            out_shape=shaped(HIDDEN_UNITS, MODEL_WIDTH, bf),
+            in_specs=[SMEM_SPEC, ANY_SPEC, ANY_SPEC],
+            out_specs=ANY_SPEC,
+            scratch_shapes=[pltpu.SemaphoreType.DMA((count,))],
+            cost_estimate=pl.CostEstimate(flops=0, bytes_accessed=4_000_000, transcendentals=0),
+        )(me_scalar, down, down2)
+        pair = [shaped(half, HALF_FFN, bf)] * 2
+        weight_scratch = [pltpu.VMEM((MODEL_WIDTH, HALF_FFN), bf)] * 2
+        og, result, back, dg0, dg0s, du0, du0s, dd = call(
+            ffn_first_kernel,
+            [
+                shaped(rows, MODEL_WIDTH, bf),
+                shaped(rows, MODEL_WIDTH, f4),
+                shaped(rows, MODEL_WIDTH, f4),
+                *pair,
+                *pair,
+                shaped(HALF_FFN, MODEL_WIDTH, bf),
+            ],
+            [spans, *o_parts, normed_two, *ffn_weights[0], w_down[:HALF_FFN]],
+            1,
+            weight_scratch,
+            6e9,
+        )
+        gu0 = scatter_group((dg0, dg0s), (du0, du0s))
+        r0, r1, r2, r3, back_middle, gain_two_grad, dg1, dg1s, du1, du1s, dd1, dd1s = call(
+            lambda *refs: ffn_second_kernel(*refs, order=order),
+            [
+                *[shaped(SPAN, MODEL_WIDTH, bf)] * 4,
+                shaped(rows, MODEL_WIDTH, f4),
+                shaped(1, MODEL_WIDTH, f4),
+                *pair,
+                *pair,
+                *[shaped(HIDDEN_UNITS // 2, MODEL_WIDTH, bf)] * 2,
+            ],
+            [
+                me_scalar, spans, og, normed_two, *ffn_weights[1], w_down[HALF_FFN:],
+                result, back, dd, middle, gain_two, place,
+            ],
+            2,
+            weight_scratch
+            + [
+                pltpu.VMEM((HALF_FFN, MODEL_WIDTH), bf),
+                pltpu.VMEM((rows, MODEL_WIDTH), f4),
+                pltpu.VMEM((rows, MODEL_WIDTH), f4),
+            ],
+            7e9,
+        )
+        gu1 = scatter_group((dg1, dg1s), (du1, du1s))
+        down_grad = scatter_z(scatter_xy(dd1, dd1s, True))
+        hidden_out = from_sequence([r0, r1, r2, r3])
+        g0, g1, g2, g3, gain_one_grad, da, das, db, dbs = call(
+            attend_back_kernel,
+            [
+                *[shaped(SPAN, MODEL_WIDTH, bf)] * 4,
+                shaped(1, MODEL_WIDTH, f4),
+                *[shaped(half, QK_WIDTH, bf)] * 4,
+            ],
+            [
+                spans, x, normed, qk, kpad, vpad, lse, attn, merged, back_middle, gain_one, place,
+                cosine, sine, wa, wa2, wb, wb2,
+            ],
+            1,
+            [
+                pltpu.VMEM((MODEL_WIDTH, QK_WIDTH), bf),
+                pltpu.VMEM((MODEL_WIDTH, QK_WIDTH), bf),
+                pltpu.VMEM((rows, 5 * LANES), bf),
+                pltpu.VMEM((rows, QK_WIDTH), f4),
+                pltpu.VMEM((rows, 2 * LANES), bf),
+                pltpu.VMEM((rows, QK_WIDTH), bf),
+            ],
+            6e9,
+        )
+        qkov = scatter_group((da, das), (db, dbs))
+        hidden_grad = from_sequence([g0, g1, g2, g3])
+        gains = lax.psum(jnp.concatenate([gain_one_grad, gain_two_grad], axis=0), axes)
+        gate_grad = jnp.concatenate([gu0[:, :HALF_FFN], gu1[:, :HALF_FFN]], axis=1)
+        up_grad = jnp.concatenate([gu0[:, HALF_FFN:], gu1[:, HALF_FFN:]], axis=1)
+        return (
+            hidden_out,
+            hidden_grad,
+            gains[0],
+            qkov[:, :Q_WIDTH].reshape(-1),
+            qkov[:, Q_WIDTH:QK_WIDTH].reshape(-1),
+            qkov[:, QK_WIDTH + MODEL_WIDTH :].reshape(-1),
+            qkov[:, QK_WIDTH : QK_WIDTH + MODEL_WIDTH].reshape(-1),
+            gains[1],
+            gate_grad.reshape(-1),
+            up_grad.reshape(-1),
+            down_grad.reshape(-1),
+        )
+
+    return on_sequence_device
+
+
+def pick_plan(mesh):
+    count = mesh.shape["dp"] * mesh.shape["seq"]
+    fits = (
+        mesh.shape["seq"] == MB * SLOTS
+        and SLOTS == 1
+        and count & (count - 1) == 0
+        and MODEL_WIDTH % count == 0
+        and (HIDDEN_UNITS // count) % 16 == 0
+    )
+    return whole_sequence_plan(mesh) if fits else on_device
+
+
 def solution(mesh):
     return jax.shard_map(
-        on_device,
+        pick_plan(mesh),
         mesh=mesh,
         in_specs=(
             P(("dp", "seq"), None),

time: 821 us -> 379 us (0.46)
  blocking collectives: 262 us -> 38 us
  waiting for transfers between devices: 261 us -> 58.6 us
  matrix products: 142 us -> 0 us
  Pallas kernels: 0 us -> 115 us
  starting transfers between devices: 1.06 us -> 67.3 us
  other arithmetic: 40.1 us -> 18.3 us
  between operations: 20.1 us -> 2.12 us
  local copies, waits for them, and re-layouts: 88.3 us -> 74.5 us
    unnamed x21 -> x0, waiting for transfers between devices: 261 us -> none
    all_gather x12 -> x0, blocking collectives: 214 us -> none  [the longest x1 44.9 us: on_device(): lax.all_gather(value_weight, ('dp', 'seq'), axis=0, tiled=True)]
    dot_general x108 -> x0, matrix products: 142 us -> none  [the longest x28 62.2 us: inner_rows(): lax.dot_general(first_arg, second_arg, (((0,), (0,)), ((), ())), preferre...]
    pallas_call x0 -> x5, Pallas kernels: none -> 115 us  [the longest x1 61 us: on_sequence_device(): pl.pallas_call(lambda *refs: place_down_kernel(*refs, order=order), out_s...]
    ppermute x0 -> x73, starting transfers between devices: none -> 67.3 us  [the longest x58 55.4 us: swap(): return lax.ppermute(v, axes, [(d, d ^ 1 << bit) for d in range(count)])]
    ppermute x0 -> x73, waiting for transfers between devices: none -> 58.6 us  [the longest x58 50.9 us: swap(): return lax.ppermute(v, axes, [(d, d ^ 1 << bit) for d in range(count)])]
    reshape x14 -> x16, local copies, waits for them, and re-layouts: 37.4 us -> 5.48 us  [the longest x1 0.74 us: on_sequence_device(): down_grad.reshape(-1)]
    unnamed x478 -> x148, local copies, waits for them, and re-layouts: 44.6 us -> 26.9 us
  transfers between devices with their start and end apart: 12 -> 73, of which waited for: 4 -> 26; matrix products, arithmetic and copies ran while one was open for 25% -> 18% of each run, Pallas kernels for 0% -> 27%
where the time goes in v1:
time: 379 us; the launch traced here: 373 us
  Pallas kernels  115 us (30%)
  local copies, waits for them, and re-layouts  74.5 us (20%)
  starting transfers between devices  67.3 us (18%)
  waiting for transfers between devices  58.6 us (15%)
  blocking collectives  38 us (10%)
  other arithmetic  18.3 us (5%)
    pallas_call x1, Pallas kernels, on_sequence_device(): pl.pallas_call(lambda *refs: place_down_kernel(*refs, order=order), out_s...  61 us
    ppermute x58, starting transfers between devices, swap(): return lax.ppermute(v, axes, [(d, d ^ 1 << bit) for d in range(count)])  55.4 us
    pallas_call x4, Pallas kernels, call(): pl.pallas_call(body, out_shape=outs, in_specs=[SMEM_SPEC] * scalars + [VM...  53.8 us
    ppermute x58, waiting for transfers between devices, swap(): return lax.ppermute(v, axes, [(d, d ^ 1 << bit) for d in range(count)])  50.9 us
    psum x1, blocking collectives, on_sequence_device(): lax.psum(jnp.concatenate([gain_one_grad, gain_two_grad], axis=0), axes)  38 us
    unnamed x148, local copies, waits for them, and re-layouts  26.9 us
    dynamic_update_slice x8, local copies, waits for them, and re-layouts, from_sequence(): out = lax.dynamic_update_slice_in_dim(out, part, (seq ^ k) * size, 0)  10.8 us
    ppermute x6, local copies, waits for them, and re-layouts, from_sequence(): part = lax.ppermute(part, 'seq', [(d, d ^ k) for d in range(n_seq)])  9.54 us
  transfers between devices with their start and end apart: 73, of which 26 were waited for; matrix products, arithmetic and copies ran while one was open for 18% of the time, Pallas kernels for 27%

profile of v1, /device:TPU:0, one launch (start us, length us, event | category | flops | bytes accessed | tf_op | source)
XLA Modules:
  0.0 373.5 jit_solution(9948199171427491709)
XLA Ops:
  2.6 2.6 collective-permute-start.1
  7.8 3.1 collective-permute-start.25
  18.8 2.9 collective-permute-start.17
  21.8 2.6 pad_add_fusion.spans.refs_1_
  24.4 5.3 %collective-permute-done.9 = bf16[18,1536]{1,0:T(8,128)(2,1)S(1)} collective-permute-done((bf16[18,1536]{1,0:T(8,128)(2,1)S(1)}, bf16[18,1536]{1,0:T(8,128)(2,1)S(1)}, u32[]{:S(2)}, u32[]{:S(2)}) %collective-permute-start.9) | collective-permute-done | bytes 55328 | tf_op jit(solution)/shard_map/ppermute | solution.py:809
  48.3 4.5 %collective-permute-done.19 = bf16[72,768]{1,0:T(8,128)(2,1)S(1)} collective-permute-done((bf16[72,768]{1,0:T(8,128)(2,1)S(1)}, bf16[72,768]{1,0:T(8,128)(2,1)S(1)}, u32[]{:S(2)}, u32[]{:S(2)}) %collective-permute-start.19) | collective-permute-done | bytes 110624 | tf_op jit(solution)/shard_map/ppermute | solution.py:809
  58.7 2.5 collective-permute-done.15
  62.7 2.5 collective-permute-done.23
  69.8 6.8 %collective-permute-done.28 = bf16[384,576]{1,0:T(8,128)(2,1)S(1)} collective-permute-done((bf16[384,576]{1,0:T(8,128)(2,1)S(1)}, bf16[384,576]{1,0:T(8,128)(2,1)S(1)}, u32[]{:S(2)}, u32[]{:S(2)}) %collective-permute-start.28) | collective-permute-done | bytes 442400 | tf_op jit(solution)/shard_map/ppermute | solution.py:809
  84.0 4.4 %collective-permute-done.7.x2 = bf16[128,576]{1,0:T(8,128)(2,1)S(1)} collective-permute-done((bf16[128,576]{1,0:T(8,128)(2,1)}, bf16[128,576]{1,0:T(8,128)(2,1)S(1)}, u32[]{:S(2)}, u32[]{:S(2)}) %collective-permute-start.7) | collective-permute-done | bytes 147488 | tf_op jit(solution)/shard_map/ppermute | solution.py:875
  92.3 15.3 %shard_map.212 = (bf16[512,576]{1,0:T(8,128)(2,1)S(1)}, bf16[512,576]{1,0:T(8,128)(2,1)S(1)}, bf16[512,768]{1,0:T(8,128)(2,1)}, bf16[6,512,128]{2,1,0:T(8,128)(2...) custom-call(s32[4]{0:T(128)S(1)} %pad_add_fusion.spans.refs_1_, ...), custom_call_target="tpu_custom_call" | custom-call | flops 4000000000 | bytes 8000000 | tf_op jit(solution)/shard_map/pallas_call | solution.py:784
  113.3 2.5 copy.71.refs_2_
  115.8 61.0 %shard_map.213 = bf16[1536,576]{1,0:T(8,128)(2,1)} custom-call(s32[1]{0:T(128)} %bitcast.refs_0_, bf16[768,576]{1,0:T(8,128)(2,1)} %copy-done.34, bf16[768,576]{1,0:T(8,128)(2,1)} %copy.71.refs_2_), custom_call_target="tpu_custom_call" | custom-call | bytes 4000000 | tf_op jit(solution)/shard_map/pallas_call | solution.py:954
  176.8 3.0 fusion.18
  181.9 9.5 %shard_map.214 = (bf16[512,576]{1,0:T(8,128)(2,1)S(1)}, f32[512,576]{1,0:T(8,128)}, f32[512,576]{1,0:T(8,128)}, bf16[288,768]{1,0:T(8,128)(2,1)S(1)}, bf16[288,7...) custom-call(s32[4]{0:T(128)S(1)} %pad_add_fusion.spans.refs_1_, ...), custom_call_target="tpu_custom_call" | custom-call | flops 6000000000 | bytes 8000000 | tf_op jit(solution)/shard_map/pallas_call | solution.py:784
  193.0 13.2 %shard_map.215 = (bf16[128,576]{1,0:T(8,128)(2,1)S(1)}, bf16[128,576]{1,0:T(8,128)(2,1)S(1)}, bf16[128,576]{1,0:T(8,128)(2,1)}, bf16[128,576]{1,0:T(8,128)(2,1)S...) custom-call(s32[1]{0:T(128)} %bitcast.refs_0_, ...), custom_call_target="tpu_custom_call" | custom-call | flops 7000000000 | bytes 8000000 | tf_op jit(solution)/shard_map/pallas_call | solution.py:784
  209.7 2.6 copy.82
  218.2 15.8 %shard_map.216 = (bf16[128,576]{1,0:T(8,128)(2,1)S(1)}, bf16[128,576]{1,0:T(8,128)(2,1)S(1)}, bf16[128,576]{1,0:T(8,128)(2,1)S(1)}, bf16[128,576]{1,0:T(8,128)(2...) custom-call(s32[4]{0:T(128)S(1)} %pad_add_fusion.spans.refs_1_, ...), custom_call_target="tpu_custom_call" | custom-call | flops 6000000000 | bytes 8000000 | tf_op jit(solution)/shard_map/pallas_call | solution.py:784
  246.3 38.0 %psum.7 = f32[2,576]{1,0:T(2,128)S(1)} all-reduce(f32[2,576]{1,0:T(2,128)S(1)} %pad_maximum_fusion.33), channel_id=1, replica_groups=mesh['dp'=8,'seq'=4] {'dp','seq'}, use_global_device_ids=true, to_apply=%region_0.1 | all-reduce | flops 1152 | bytes 9216 | tf_op jit(solution)/shard_map/psum | solution.py:1030
  327.7 2.7 collective-permute-done.45
  336.2 2.4 collective-permute-start.58
  346.2 2.4 collective-permute-start.67
  356.9 5.2 %collective-permute-done.70 = bf16[192,576]{1,0:T(8,128)(2,1)S(1)} collective-permute-done((bf16[192,576]{1,0:T(8,128)(2,1)S(1)}, bf16[192,576]{1,0:T(8,128)(2,1)S(1)}, u32[]{:S(2)}, u32[]{:S(2)}) %collective-permute-start.70) | collective-permute-done | bytes 221216 | tf_op jit(solution)/shard_map/ppermute | solution.py:809
  362.3 5.0 %collective-permute-done.71 = bf16[96,576]{1,0:T(8,128)(2,1)S(1)} collective-permute-done((bf16[96,576]{1,0:T(8,128)(2,1)S(1)}, bf16[96,576]{1,0:T(8,128)(2,1)S(1)}, u32[]{:S(2)}, u32[]{:S(2)}) %collective-permute-start.71) | collective-permute-done | bytes 110624 | tf_op jit(solution)/shard_map/ppermute | solution.py:809
  (430 shorter events, 155.6 us)
Async XLA Ops:
  2.1 16.6 %collective-permute-start = (s32[1]{0:T(128)}, s32[1]{0:T(128)}, u32[]{:S(2)}, u32[]{:S(2)}) collective-permute-start(s32[1]{0:T(128)} %get-tuple-element.152), channel_id=1, source_target_pairs={{0,1},{1,0},{2,3},{3,2},{4,5},{5,4},{6,7},{7,6},{8,9},{9,8},{10,11... | collective-permute-start | bytes 20 | tf_op jit(solution)/shard_map/ppermute | solution.py:875
  2.6 16.2 %collective-permute-start.1 = (s32[1]{0:T(128)}, s32[1]{0:T(128)}, u32[]{:S(2)}, u32[]{:S(2)}) collective-permute-start(s32[1]{0:T(128)} %get-tuple-element.154), channel_id=1, source_target_pairs={{0,2},{1,3},{2,0},{3,1},{4,6},{5,7},{6,4},{7,5},{8,10},{9,11},{10,... | collective-permute-start | bytes 20 | tf_op jit(solution)/shard_map/ppermute | solution.py:875
  5.1 16.6 %collective-permute-start.2 = (s32[1]{0:T(128)}, s32[1]{0:T(128)}, u32[]{:S(2)}, u32[]{:S(2)}) collective-permute-start(s32[1]{0:T(128)} %get-tuple-element.153), channel_id=1, source_target_pairs={{0,3},{1,2},{2,1},{3,0},{4,7},{5,6},{6,5},{7,4},{8,11},{9,10},{10,... | collective-permute-start | bytes 20 | tf_op jit(solution)/shard_map/ppermute | solution.py:875
  7.5 75.7 %collective-permute-start.6 = (bf16[128,576]{1,0:T(8,128)(2,1)}, bf16[128,576]{1,0:T(8,128)(2,1)S(1)}, u32[]{:S(2)}, u32[]{:S(2)}) collective-permute-start(bf16[128,576]{1,0:T(8,128)(2,1)} %copy.89), channel_id=1, source_target_pairs={{0,1},{1,0},{2,3},{3,2},{4,5},{5,4},{6,7},{7,6},{8,9},{9,8},{10,11... | collective-permute-start | bytes 442376 | tf_op jit(solution)/shard_map/ppermute | solution.py:875
  7.8 24.1 %collective-permute-start.25 = (bf16[48,576]{1,0:T(8,128)(2,1)S(1)}, bf16[48,576]{1,0:T(8,128)(2,1)S(1)}, u32[]{:S(2)}, u32[]{:S(2)}) collective-permute-start(bf16[48,576]{1,0:T(8,128)(2,1)S(1)} %reshape.204), channel_id=1, source_target_pairs={{0,16},{1,17},{2,18},{3,19},{4,20},{5,21},{6,22},{7,23},{8,24},{9,... | collective-permute-start | bytes 165896 | tf_op jit(solution)/shard_map/ppermute | solution.py:809
  18.8 12.1 %collective-permute-start.17 = (bf16[18,1536]{1,0:T(8,128)(2,1)S(1)}, bf16[18,1536]{1,0:T(8,128)(2,1)S(1)}, u32[]{:S(2)}, u32[]{:S(2)}) collective-permute-start(bf16[18,1536]{1,0:T(8,128)(2,1)S(1)} %pad_maximum_fusion.31), channel_id=1, source_target_pairs={{0,16},{1,17},{2,18},{3,19},{4,20},{5,21},{6,22},{7,23},{8,24},{9,... | collective-permute-start | bytes 165896 | tf_op jit(solution)/shard_map/ppermute | solution.py:809
  41.9 15.7 %collective-permute-start.27 = (bf16[192,576]{1,0:T(8,128)(2,1)S(1)}, bf16[192,576]{1,0:T(8,128)(2,1)S(1)}, u32[]{:S(2)}, u32[]{:S(2)}) collective-permute-start(bf16[192,576]{1,0:T(8,128)(2,1)S(1)} %pad_maximum_fusion.11), channel_id=1, source_target_pairs={{0,4},{1,5},{2,6},{3,7},{4,0},{5,1},{6,2},{7,3},{8,12},{9,13},{10,... | collective-permute-start | bytes 663560 | tf_op jit(solution)/shard_map/ppermute | solution.py:809
  55.0 23.2 %collective-permute-start.12 = (bf16[144,768]{1,0:T(8,128)(2,1)}, bf16[144,768]{1,0:T(8,128)(2,1)}, u32[]{:S(2)}, u32[]{:S(2)}) collective-permute-start(bf16[144,768]{1,0:T(8,128)(2,1)} %pad_maximum_fusion.13), channel_id=1, source_target_pairs={{0,2},{1,3},{2,0},{3,1},{4,6},{5,7},{6,4},{7,5},{8,10},{9,11},{10,... | collective-permute-start | bytes 663560 | tf_op jit(solution)/shard_map/ppermute | solution.py:809
  57.6 22.2 %collective-permute-start.20 = (bf16[144,768]{1,0:T(8,128)(2,1)}, bf16[144,768]{1,0:T(8,128)(2,1)}, u32[]{:S(2)}, u32[]{:S(2)}) collective-permute-start(bf16[144,768]{1,0:T(8,128)(2,1)} %pad_maximum_fusion.16), channel_id=1, source_target_pairs={{0,2},{1,3},{2,0},{3,1},{4,6},{5,7},{6,4},{7,5},{8,10},{9,11},{10,... | collective-permute-start | bytes 663560 | tf_op jit(solution)/shard_map/ppermute | solution.py:809
  67.6 13.5 %collective-permute-start.33 = (bf16[144,768]{1,0:T(8,128)(2,1)}, bf16[144,768]{1,0:T(8,128)(2,1)}, u32[]{:S(2)}, u32[]{:S(2)}) collective-permute-start(bf16[144,768]{1,0:T(8,128)(2,1)} %pad_maximum_fusion.19), channel_id=1, source_target_pairs={{0,2},{1,3},{2,0},{3,1},{4,6},{5,7},{6,4},{7,5},{8,10},{9,11},{10,... | collective-permute-start | bytes 663560 | tf_op jit(solution)/shard_map/ppermute | solution.py:809
  76.6 15.1 %collective-permute-start.16 = (bf16[288,768]{1,0:T(8,128)(2,1)S(1)}, bf16[288,768]{1,0:T(8,128)(2,1)}, u32[]{:S(2)}, u32[]{:S(2)}) collective-permute-start(bf16[288,768]{1,0:T(8,128)(2,1)S(1)} %pad_maximum_fusion.3.wb), channel_id=1, source_target_pairs={{0,1},{1,0},{2,3},{3,2},{4,5},{5,4},{6,7},{7,6},{8,9},{9,8},{10,11... | collective-permute-start | bytes 1327112 | tf_op jit(solution)/shard_map/ppermute | solution.py:809
  78.3 33.4 %collective-permute-start.29 = (bf16[768,576]{0,1:T(8,128)(2,1)}, bf16[768,576]{0,1:T(8,128)(2,1)S(1)}, u32[]{:S(2)}, u32[]{:S(2)}) collective-permute-start(bf16[768,576]{0,1:T(8,128)(2,1)} %copy.70), channel_id=1, source_target_pairs={{0,1},{1,0},{2,3},{3,2},{4,5},{5,4},{6,7},{7,6},{8,9},{9,8},{10,11... | collective-permute-start | bytes 2654216 | tf_op jit(solution)/shard_map/ppermute | solution.py:809
  88.4 91.4 %collective-permute-start.3 = (bf16[128,576]{1,0:T(8,128)(2,1)}, bf16[128,576]{1,0:T(8,128)(2,1)}, u32[]{:S(2)}, u32[]{:S(2)}) collective-permute-start(bf16[128,576]{1,0:T(8,128)(2,1)} %copy.85), channel_id=1, source_target_pairs={{0,1},{1,0},{2,3},{3,2},{4,5},{5,4},{6,7},{7,6},{8,9},{9,8},{10,11... | collective-permute-start | bytes 442376 | tf_op jit(solution)/shard_map/ppermute | solution.py:875
  90.6 89.5 %collective-permute-start.4 = (bf16[128,576]{1,0:T(8,128)(2,1)}, bf16[128,576]{1,0:T(8,128)(2,1)}, u32[]{:S(2)}, u32[]{:S(2)}) collective-permute-start(bf16[128,576]{1,0:T(8,128)(2,1)} %copy.86), channel_id=1, source_target_pairs={{0,2},{1,3},{2,0},{3,1},{4,6},{5,7},{6,4},{7,5},{8,10},{9,11},{10,... | collective-permute-start | bytes 442376 | tf_op jit(solution)/shard_map/ppermute | solution.py:875
  91.7 89.2 %collective-permute-start.24 = (bf16[288,768]{1,0:T(8,128)(2,1)S(1)}, bf16[288,768]{1,0:T(8,128)(2,1)}, u32[]{:S(2)}, u32[]{:S(2)}) collective-permute-start(bf16[288,768]{1,0:T(8,128)(2,1)S(1)} %pad_maximum_fusion.5.wu1), channel_id=1, source_target_pairs={{0,1},{1,0},{2,3},{3,2},{4,5},{5,4},{6,7},{7,6},{8,9},{9,8},{10,11... | collective-permute-start | bytes 1327112 | tf_op jit(solution)/shard_map/ppermute | solution.py:809
  91.9 89.1 %collective-permute-start.21 = (bf16[288,768]{1,0:T(8,128)(2,1)S(1)}, bf16[288,768]{1,0:T(8,128)(2,1)}, u32[]{:S(2)}, u32[]{:S(2)}) collective-permute-start(bf16[288,768]{1,0:T(8,128)(2,1)S(1)} %pad_maximum_fusion.4.wg1), channel_id=1, source_target_pairs={{0,1},{1,0},{2,3},{3,2},{4,5},{5,4},{6,7},{7,6},{8,9},{9,8},{10,11... | collective-permute-start | bytes 1327112 | tf_op jit(solution)/shard_map/ppermute | solution.py:809
  112.6 67.7 %collective-permute-start.5 = (bf16[128,576]{1,0:T(8,128)(2,1)}, bf16[128,576]{1,0:T(8,128)(2,1)S(1)}, u32[]{:S(2)}, u32[]{:S(2)}) collective-permute-start(bf16[128,576]{1,0:T(8,128)(2,1)} %copy.87), channel_id=1, source_target_pairs={{0,3},{1,2},{2,1},{3,0},{4,7},{5,6},{6,5},{7,4},{8,11},{9,10},{10,... | collective-permute-start | bytes 442376 | tf_op jit(solution)/shard_map/ppermute | solution.py:875
  179.8 12.4 %collective-permute-start.37 = (bf16[288,768]{1,0:T(8,128)(2,1)S(1)}, bf16[288,768]{1,0:T(8,128)(2,1)S(1)}, u32[]{:S(2)}, u32[]{:S(2)}) collective-permute-start(bf16[288,768]{1,0:T(8,128)(2,1)S(1)} %pad_maximum_fusion.7.refs_6_), channel_id=1, source_target_pairs={{0,1},{1,0},{2,3},{3,2},{4,5},{5,4},{6,7},{7,6},{8,9},{9,8},{10,11... | collective-permute-start | bytes 1327112 | tf_op jit(solution)/shard_map/ppermute | solution.py:809
  212.3 130.3 %collective-permute-start.68 = (bf16[768,576]{0,1:T(8,128)(2,1)}, bf16[768,576]{0,1:T(8,128)(2,1)}, u32[]{:S(2)}, u32[]{:S(2)}) collective-permute-start(bf16[768,576]{0,1:T(8,128)(2,1)} %copy.82), channel_id=1, source_target_pairs={{0,1},{1,0},{2,3},{3,2},{4,5},{5,4},{6,7},{7,6},{8,9},{9,8},{10,11... | collective-permute-start | bytes 2654216 | tf_op jit(solution)/shard_map/ppermute | solution.py:809
  212.7 95.6 %collective-permute-start.55 = (bf16[288,768]{1,0:T(8,128)(2,1)}, bf16[288,768]{1,0:T(8,128)(2,1)}, u32[]{:S(2)}, u32[]{:S(2)}) collective-permute-start(bf16[288,768]{1,0:T(8,128)(2,1)} %copy-done.16), channel_id=1, source_target_pairs={{0,1},{1,0},{2,3},{3,2},{4,5},{5,4},{6,7},{7,6},{8,9},{9,8},{10,11... | collective-permute-start | bytes 1327112 | tf_op jit(solution)/shard_map/ppermute | solution.py:809
  212.9 96.6 %collective-permute-start.52 = (bf16[288,768]{1,0:T(8,128)(2,1)}, bf16[288,768]{1,0:T(8,128)(2,1)}, u32[]{:S(2)}, u32[]{:S(2)}) collective-permute-start(bf16[288,768]{1,0:T(8,128)(2,1)} %copy-done.11), channel_id=1, source_target_pairs={{0,1},{1,0},{2,3},{3,2},{4,5},{5,4},{6,7},{7,6},{8,9},{9,8},{10,11... | collective-permute-start | bytes 1327112 | tf_op jit(solution)/shard_map/ppermute | solution.py:809
  239.3 45.6 %collective-permute-start.41 = (bf16[128,576]{1,0:T(8,128)(2,1)}, bf16[128,576]{1,0:T(8,128)(2,1)}, u32[]{:S(2)}, u32[]{:S(2)}) collective-permute-start(bf16[128,576]{1,0:T(8,128)(2,1)} %copy-done.23), channel_id=1, source_target_pairs={{0,1},{1,0},{2,3},{3,2},{4,5},{5,4},{6,7},{7,6},{8,9},{9,8},{10,11... | collective-permute-start | bytes 442376 | tf_op jit(solution)/shard_map/ppermute | solution.py:884
  239.5 48.9 %collective-permute-start.42 = (bf16[128,576]{1,0:T(8,128)(2,1)}, bf16[128,576]{1,0:T(8,128)(2,1)}, u32[]{:S(2)}, u32[]{:S(2)}) collective-permute-start(bf16[128,576]{1,0:T(8,128)(2,1)} %copy-done.22), channel_id=1, source_target_pairs={{0,2},{1,3},{2,0},{3,1},{4,6},{5,7},{6,4},{7,5},{8,10},{9,11},{10,... | collective-permute-start | bytes 442376 | tf_op jit(solution)/shard_map/ppermute | solution.py:884
  319.6 12.3 %collective-permute-start.48 = (bf16[144,768]{1,0:T(8,128)(2,1)S(1)}, bf16[144,768]{1,0:T(8,128)(2,1)S(1)}, u32[]{:S(2)}, u32[]{:S(2)}) collective-permute-start(bf16[144,768]{1,0:T(8,128)(2,1)S(1)} %pad_maximum_fusion.21), channel_id=1, source_target_pairs={{0,4},{1,5},{2,6},{3,7},{4,0},{5,1},{6,2},{7,3},{8,12},{9,13},{10,... | collective-permute-start | bytes 663560 | tf_op jit(solution)/shard_map/ppermute | solution.py:809
  (117 other events, 1026.0 us)
